TPU v7x, 32 devices: a whole 2x2x4 slice. The times are simulated.
32 devices in a mesh: wide: 8 (over y, x, core), tensor: 4 (over z).
Axes of the slice: x: 2, y: 2, z: 4, core: 2. Of those that a mesh axis runs over, the one named last changes fastest.
Arguments:
- pixels: bfloat16 [1, 16, 128, 1024], P(None, 'wide', None, 'tensor'), may hold values from -25 to 25
- text_states: bfloat16 [1, 128, 4096], replicated, may hold values from -6 to 6
- text_length: int32 [1], replicated, may hold values from 17 to 128
- timestep: int32 [1], replicated, may hold values from 0 to 999
- conv_weights: bfloat16 [2, 9, 1024, 1024], P(None, None, 'wide', 'tensor'), may hold values from -0.0625 to 0.0625
- film_time: bfloat16 [1024, 2, 1024], P('wide', None, 'tensor'), may hold values from -0.1875 to 0.1875
- film_text: bfloat16 [4096, 2, 1024], P('wide', None, 'tensor'), may hold values from -0.375 to 0.375
- group_gain: float32 [2, 1024], P(None, 'tensor'), may hold values from 0.25 to 1.75
- group_bias: float32 [2, 1024], P(None, 'tensor'), may hold values from -3 to 3
- layer_gain: float32 [1024], P('tensor'), may hold values from 0.25 to 1.75
- layer_bias: float32 [1024], P('tensor'), may hold values from -3 to 3
- attn_in: bfloat16 [4, 1024, 1024], P(None, 'wide', 'tensor'), may hold values from -0.25 to 0.25
- text_kv: bfloat16 [2, 4096, 1024], P(None, 'wide', 'tensor'), may hold values from -0.125 to 0.125
- out_self: bfloat16 [1024, 1024], P('tensor', 'wide'), may hold values from -3 to 3
- out_cross: bfloat16 [1024, 1024], P('tensor', 'wide'), may hold values from -0.25 to 0.25
- cotangent: float32 [1, 16, 128, 1024], P(None, 'wide', None, 'tensor'), may hold values from -6 to 6
Outputs:
- result: float32 [1, 16, 128, 1024], P(None, 'wide', None, 'tensor')
- pixels_grad: float32 [1, 16, 128, 1024], P(None, 'wide', None, 'tensor')
- conv_grad: float32 [2, 9, 1024, 1024], P(None, None, 'wide', 'tensor')
- film_time_grad: float32 [1024, 2, 1024], P('wide', None, 'tensor')
- film_text_grad: float32 [4096, 2, 1024], P('wide', None, 'tensor')
- group_gain_grad: float32 [2, 1024], P(None, 'tensor')
- group_bias_grad: float32 [2, 1024], P(None, 'tensor')
- layer_gain_grad: float32 [1024], P('tensor')
- layer_bias_grad: float32 [1024], P('tensor')
- attn_in_grad: float32 [4, 1024, 1024], P(None, 'wide', 'tensor')
- text_kv_grad: float32 [2, 4096, 1024], P(None, 'wide', 'tensor')
- out_self_grad: float32 [1024, 1024], P('tensor', 'wide')
- out_cross_grad: float32 [1024, 1024], P('tensor', 'wide')
All inputs are finite; a program needn't handle non-finite values.
Results may differ from a plain program's by a relative error of at most 0.02.
Values may be sent and summed in bfloat16 or wider, within the bound.
No kernel may reach another device: no remote copies, remote signals or barrier semaphores. Data moves between devices by JAX's collectives and lax.ppermute only.
A program may use at most 192 MiB of HBM per device.

v0:
```python
import math

import jax
import jax.numpy as jnp
from jax import lax
from jax.sharding import PartitionSpec as P

C = 1024
GROUPS = 32
HEAD_DIM = 128
TEXT = 128
TEMB = 1024


root_half = 1.0 / math.sqrt(2.0)
highest = lax.Precision.HIGHEST


def extended(cells, sides, width):
    for axis, dim in sides:
        count = lax.axis_size(axis)
        ends = count - 1
        head = lax.slice_in_dim(cells, 0, width, axis=dim)
        tail = lax.slice_in_dim(cells, cells.shape[dim] - width, cells.shape[dim], axis=dim)
        cells = jnp.concatenate(
            [
                lax.ppermute(tail, axis, [(i, (i + 1) % count) for i in range(ends)]),
                cells,
                lax.ppermute(head, axis, [((i + 1) % count, i) for i in range(ends)]),
            ],
            axis=dim,
        )
    return cells


def sinusoid(steps):
    half_width = TEMB // 2
    frequency = jnp.exp(-math.log(10000.0) * jnp.arange(half_width, dtype=jnp.float32) / half_width)
    angles = steps.astype(jnp.float32)[:, None] * frequency[None, :]
    return jnp.concatenate([jnp.cos(angles), jnp.sin(angles)], axis=1)


def silu_slope(values):
    logistic = jax.nn.sigmoid(values)
    return logistic * (1.0 + values * (1.0 - logistic))


def wide_total(first, second):
    return lax.psum((first, second), "wide")


def token_total(first, second):
    return lax.psum((first, second), "tensor")


def rows_of(values):
    return extended(values, (("wide", 1),), 1)


def full_channels(values):
    return lax.all_gather(values, "tensor", axis=3, tiled=True)


def own_part(values):
    return lax.psum_scatter(
        values.astype(jnp.bfloat16), "tensor", scatter_dimension=3, tiled=True
    ).astype(jnp.float32)


def spread(values):
    framed = rows_of(full_channels(values))
    return jnp.pad(framed, ((0, 0), (0, 0), (1, 1), (0, 0)))


def group_mean(values, count):
    map_count = values.shape[0]
    per_group = C // GROUPS
    summed = jnp.sum(values.reshape(map_count, -1, per_group), axis=2) / count
    return jnp.repeat(summed, per_group, axis=1)[:, None, None, :]


def group_forward(values, count):
    sums, squares = wide_total(jnp.sum(values, axis=(1, 2)), jnp.sum(values * values, axis=(1, 2)))
    center = group_mean(sums, count)
    inverse = lax.rsqrt(group_mean(squares, count) - center * center + 1e-05)
    return ((values - center) * inverse, center, inverse)


def group_backward(grad_normed, scaled, gain, inverse, count, extra_first, extra_second):
    map_count = scaled.shape[0]
    first = jnp.sum(grad_normed * scaled, axis=(1, 2))
    second = jnp.sum(grad_normed, axis=(1, 2))
    first_all, second_all = wide_total(
        jnp.concatenate([first, extra_first], axis=0),
        jnp.concatenate([second, extra_second], axis=0),
    )
    gain_grad = jnp.sum(first_all[:map_count], axis=0)
    bias_grad = jnp.sum(second_all[:map_count], axis=0)
    dot_mean = group_mean(gain * first_all[:map_count], count)
    plain_mean = group_mean(gain * second_all[:map_count], count)
    grad_values = inverse * (grad_normed * gain - plain_mean - scaled * dot_mean)
    return (grad_values, gain_grad, bias_grad, first_all[map_count:], second_all[map_count:])


def convolve(framed, kernel):
    row_count = framed.shape[1] - 2
    col_count = framed.shape[2] - 2
    summed = None
    for position in range(9):
        window = framed[
            :, position // 3 : position // 3 + row_count, position % 3 : position % 3 + col_count, :
        ]
        contribution = jnp.einsum(
            "mrwc,cd->mrwd", window, kernel[position], preferred_element_type=jnp.float32
        )
        summed = contribution if position == 0 else summed + contribution
    return summed


def kernel_grad(framed, grad_low):
    row_count = grad_low.shape[1]
    col_count = grad_low.shape[2]
    return jnp.stack(
        [
            jnp.einsum(
                "mrwc,mrwd->cd",
                framed[
                    :,
                    position // 3 : position // 3 + row_count,
                    position % 3 : position % 3 + col_count,
                    :,
                ],
                grad_low,
                preferred_element_type=jnp.float32,
            )
            for position in range(9)
        ]
    )


def input_grad(grad_low, kernel):
    row_count = grad_low.shape[1]
    col_count = grad_low.shape[2]
    framed = jnp.pad(rows_of(grad_low), ((0, 0), (0, 0), (1, 1), (0, 0)))
    summed = None
    for position in range(9):
        top_row = 2 - position // 3
        left_col = 2 - position % 3
        window = framed[:, top_row : top_row + row_count, left_col : left_col + col_count, :]
        contribution = jnp.einsum(
            "mrwd,cd->mrwc", window, kernel[position], preferred_element_type=jnp.float32
        )
        summed = contribution if position == 0 else summed + contribution
    return summed


def key_blocks(array, block_rows):
    map_count = array.shape[0]
    length = array.shape[1]
    shaped = array.reshape((map_count, length // block_rows, block_rows) + array.shape[2:])
    return jnp.moveaxis(shaped, 1, 0)


def attend_forward(query, keys, values):
    score_scale = HEAD_DIM ** (-0.5)
    map_count, query_count, head_count = (query.shape[0], query.shape[1], query.shape[2])
    start_state = (
        jnp.full((map_count, query_count, head_count), -1e30, jnp.float32),
        jnp.zeros((map_count, query_count, head_count), jnp.float32),
        jnp.zeros(query.shape, jnp.float32),
    )
    pieces = (
        lax.all_gather(keys, "wide", axis=1, tiled=True),
        lax.all_gather(values, "wide", axis=1, tiled=True),
    )
    block_rows = math.gcd(pieces[0].shape[1], 1024)

    def attend_one_block(inner_state, blocks):
        running_max, weight_sum, weighted = inner_state
        key_block, value_block = blocks
        scores = (
            jnp.einsum("mqhd,mkhd->mqhk", query, key_block, preferred_element_type=jnp.float32)
            * score_scale
        )
        raised = jnp.maximum(running_max, jnp.max(scores, axis=-1))
        rescale = jnp.exp(running_max - raised)
        weights = jnp.exp(scores - raised[..., None])
        weight_sum = weight_sum * rescale + jnp.sum(weights, axis=-1)
        weighted = weighted * rescale[..., None] + jnp.einsum(
            "mqhk,mkhd->mqhd",
            weights.astype(jnp.bfloat16),
            value_block,
            preferred_element_type=jnp.float32,
        )
        return ((raised, weight_sum, weighted), None)

    outcome, unused = lax.scan(
        attend_one_block,
        start_state,
        (key_blocks(pieces[0], block_rows), key_blocks(pieces[1], block_rows)),
    )
    running_max, weight_sum, weighted = outcome
    return (weighted / weight_sum[..., None], running_max + jnp.log(weight_sum))


def query_grads(query, grad_out, log_sums, deltas, keys, values):
    score_scale = HEAD_DIM ** (-0.5)
    pieces = (
        lax.all_gather(keys, "wide", axis=1, tiled=True),
        lax.all_gather(values, "wide", axis=1, tiled=True),
    )
    block_rows = math.gcd(pieces[0].shape[1], 1024)

    def query_one_block(grad_sum, blocks):
        key_block, value_block = blocks
        scores = (
            jnp.einsum("mqhd,mkhd->mqhk", query, key_block, preferred_element_type=jnp.float32)
            * score_scale
        )
        probs = jnp.exp(scores - log_sums[..., None])
        grad_probs = jnp.einsum(
            "mqhd,mkhd->mqhk", grad_out, value_block, preferred_element_type=jnp.float32
        )
        grad_scores = (probs * (grad_probs - deltas[..., None])).astype(jnp.bfloat16)
        grad_sum = (
            grad_sum
            + jnp.einsum(
                "mqhk,mkhd->mqhd", grad_scores, key_block, preferred_element_type=jnp.float32
            )
            * score_scale
        )
        return (grad_sum, None)

    outcome, unused = lax.scan(
        query_one_block,
        jnp.zeros(query.shape, jnp.float32),
        (key_blocks(pieces[0], block_rows), key_blocks(pieces[1], block_rows)),
    )
    return outcome


def key_grads(keys, values, query_wide, grad_wide, log_sums, deltas):
    score_scale = HEAD_DIM ** (-0.5)
    start_state = (jnp.zeros(keys.shape, jnp.float32), jnp.zeros(keys.shape, jnp.float32))
    pieces = (
        lax.all_gather(query_wide, "wide", axis=1, tiled=True),
        lax.all_gather(grad_wide, "wide", axis=1, tiled=True),
        lax.all_gather(log_sums, "wide", axis=1, tiled=True),
        lax.all_gather(deltas, "wide", axis=1, tiled=True),
    )
    block_rows = math.gcd(pieces[0].shape[1], 1024)

    def key_one_block(sums, blocks):
        grad_keys, grad_values = sums
        query_block, grad_block, log_block, delta_block = blocks
        query_low = query_block.astype(jnp.bfloat16)
        grad_low = grad_block.astype(jnp.bfloat16)
        scores = (
            jnp.einsum("mqhd,mkhd->mqhk", query_low, keys, preferred_element_type=jnp.float32)
            * score_scale
        )
        probs = jnp.exp(scores - log_block[..., None])
        grad_values = grad_values + jnp.einsum(
            "mqhk,mqhd->mkhd",
            probs.astype(jnp.bfloat16),
            grad_low,
            preferred_element_type=jnp.float32,
        )
        grad_probs = jnp.einsum(
            "mqhd,mkhd->mqhk", grad_low, values, preferred_element_type=jnp.float32
        )
        grad_scores = (probs * (grad_probs - delta_block[..., None])).astype(jnp.bfloat16)
        grad_keys = (
            grad_keys
            + jnp.einsum(
                "mqhk,mqhd->mkhd", grad_scores, query_low, preferred_element_type=jnp.float32
            )
            * score_scale
        )
        return ((grad_keys, grad_values), None)

    blocks = (
        key_blocks(pieces[0], block_rows),
        key_blocks(pieces[1], block_rows),
        key_blocks(pieces[2], block_rows),
        key_blocks(pieces[3], block_rows),
    )
    outcome, unused = lax.scan(key_one_block, start_state, blocks)
    return outcome


def shards(
    pixels,
    text_states,
    text_length,
    timestep,
    conv_weights,
    film_time,
    film_text,
    group_gain,
    group_bias,
    layer_gain,
    layer_bias,
    attn_in,
    text_kv,
    out_self,
    out_cross,
    cotangent,
):
    map_count, row_count, col_count, width_own = pixels.shape
    head_count = width_own // HEAD_DIM
    token_count = row_count * col_count
    pixel_count = row_count * lax.axis_size("wide") * col_count * (C // GROUPS)
    score_scale = HEAD_DIM ** (-0.5)
    gathered = (
        lax.all_gather(conv_weights, "wide", axis=2, tiled=True),
        lax.all_gather(attn_in, "wide", axis=1, tiled=True),
        lax.all_gather(out_self, "wide", axis=1, tiled=True),
        lax.all_gather(out_cross, "wide", axis=1, tiled=True),
    )
    kernels, in_maps, self_out, cross_out = gathered
    features = sinusoid(timestep).astype(jnp.bfloat16)
    present = jnp.arange(TEXT)[None, :] < text_length[:, None]
    pooled = jnp.einsum(
        "mtx,mt->mx", text_states, present.astype(jnp.bfloat16), preferred_element_type=jnp.float32
    )
    pooled = (pooled / text_length.astype(jnp.float32)[:, None]).astype(jnp.bfloat16)
    wide_index = lax.axis_index("wide")
    time_rows = film_time.shape[0]
    text_rows = film_text.shape[0]
    own_features = lax.dynamic_slice_in_dim(features, wide_index * time_rows, time_rows, 1)
    own_pooled = lax.dynamic_slice_in_dim(pooled, wide_index * text_rows, text_rows, 1)
    own_text = lax.dynamic_slice_in_dim(text_states, wide_index * text_rows, text_rows, 2)
    film_term = jnp.einsum(
        "mk,ksc->msc", own_features, film_time, preferred_element_type=jnp.float32
    ) + jnp.einsum("mk,ksc->msc", own_pooled, film_text, preferred_element_type=jnp.float32)
    text_term = jnp.einsum("mtx,pxd->pmtd", own_text, text_kv, preferred_element_type=jnp.float32)
    film, text_total = lax.psum((film_term, text_term), "wide")
    text_proj = text_total.astype(jnp.bfloat16)
    film_scale = film[:, 0][:, None, None, :]
    film_shift = film[:, 1][:, None, None, :]
    source = pixels.astype(jnp.float32)
    first_scaled, first_center, first_inverse = group_forward(source, pixel_count)
    first_normed = first_scaled * group_gain[0] + group_bias[0]
    first_framed = spread(jax.nn.silu(first_normed).astype(jnp.bfloat16))
    inner = convolve(first_framed, kernels[0])
    lifted = inner * (1.0 + film_scale) + film_shift
    second_scaled, second_center, second_inverse = group_forward(lifted, pixel_count)
    second_normed = second_scaled * group_gain[1] + group_bias[1]
    second_framed = spread(jax.nn.silu(second_normed).astype(jnp.bfloat16))
    middle = (source + convolve(second_framed, kernels[1])) * root_half
    token_sum, token_square = token_total(jnp.sum(middle, axis=3), jnp.sum(middle * middle, axis=3))
    token_center = token_sum / C
    token_inverse = lax.rsqrt(token_square / C - token_center * token_center + 1e-05)[..., None]
    token_scaled = (middle - token_center[..., None]) * token_inverse
    normed = full_channels((token_scaled * layer_gain + layer_bias).astype(jnp.bfloat16)).reshape(
        map_count, token_count, C
    )
    projected = jnp.einsum(
        "mnc,pcd->pmnd", normed, in_maps, preferred_element_type=jnp.float32
    ).astype(jnp.bfloat16)
    heads_shape = (map_count, token_count, head_count, HEAD_DIM)
    text_shape = (map_count, TEXT, head_count, HEAD_DIM)
    query = projected[0].reshape(heads_shape)
    keys = projected[1].reshape(heads_shape)
    values = projected[2].reshape(heads_shape)
    cross_query = projected[3].reshape(heads_shape)
    cross_keys = text_proj[0].reshape(text_shape)
    cross_values = text_proj[1].reshape(text_shape)
    attended, log_sums = attend_forward(query, keys, values)
    attended_low = attended.astype(jnp.bfloat16).reshape(map_count, token_count, width_own)
    cross_scores = (
        jnp.einsum("mqhd,mkhd->mqhk", cross_query, cross_keys, preferred_element_type=jnp.float32)
        * score_scale
    )
    cross_probs = jax.nn.softmax(jnp.where(present[:, None, None, :], cross_scores, -1e30), axis=-1)
    crossed = jnp.einsum(
        "mqhk,mkhd->mqhd",
        cross_probs.astype(jnp.bfloat16),
        cross_values,
        preferred_element_type=jnp.float32,
    )
    crossed_low = crossed.astype(jnp.bfloat16).reshape(map_count, token_count, width_own)
    mixed = jnp.einsum(
        "mnh,hc->mnc", attended_low, self_out, preferred_element_type=jnp.float32
    ) + jnp.einsum("mnh,hc->mnc", crossed_low, cross_out, preferred_element_type=jnp.float32)
    result = middle + own_part(mixed.reshape(map_count, row_count, col_count, C))
    regathered = (
        lax.all_gather(conv_weights, "wide", axis=2, tiled=True),
        lax.all_gather(attn_in, "wide", axis=1, tiled=True),
        lax.all_gather(out_self, "wide", axis=1, tiled=True),
        lax.all_gather(out_cross, "wide", axis=1, tiled=True),
    )
    kernels, in_maps, self_out, cross_out = regathered
    grad_full = full_channels(cotangent.astype(jnp.bfloat16)).reshape(map_count, token_count, C)
    out_self_part = jnp.einsum(
        "mnh,mnc->hc", attended_low, grad_full, preferred_element_type=jnp.float32
    )
    out_cross_part = jnp.einsum(
        "mnh,mnc->hc", crossed_low, grad_full, preferred_element_type=jnp.float32
    )
    grad_attended = (
        jnp.einsum("mnc,hc->mnh", grad_full, self_out, preferred_element_type=jnp.float32)
        .astype(jnp.bfloat16)
        .reshape(heads_shape)
    )
    grad_crossed = (
        jnp.einsum("mnc,hc->mnh", grad_full, cross_out, preferred_element_type=jnp.float32)
        .astype(jnp.bfloat16)
        .reshape(heads_shape)
    )
    deltas = jnp.sum(grad_attended.astype(jnp.float32) * attended, axis=-1)
    grad_query = query_grads(query, grad_attended, log_sums, deltas, keys, values).astype(
        jnp.bfloat16
    )
    grad_keys, grad_values = key_grads(
        keys, values, query.astype(jnp.float32), grad_attended.astype(jnp.float32), log_sums, deltas
    )
    grad_cross_probs = jnp.einsum(
        "mqhd,mkhd->mqhk", grad_crossed, cross_values, preferred_element_type=jnp.float32
    )
    grad_cross_scores = cross_probs * (
        grad_cross_probs - jnp.sum(cross_probs * grad_cross_probs, axis=-1, keepdims=True)
    )
    grad_cross_low = grad_cross_scores.astype(jnp.bfloat16)
    grad_cross_query = (
        jnp.einsum(
            "mqhk,mkhd->mqhd", grad_cross_low, cross_keys, preferred_element_type=jnp.float32
        )
        * score_scale
    ).astype(jnp.bfloat16)
    grad_cross_keys = (
        jnp.einsum(
            "mqhk,mqhd->mkhd", grad_cross_low, cross_query, preferred_element_type=jnp.float32
        )
        * score_scale
    )
    grad_cross_values = jnp.einsum(
        "mqhk,mqhd->mkhd",
        cross_probs.astype(jnp.bfloat16),
        grad_crossed,
        preferred_element_type=jnp.float32,
    )
    text_grads = jnp.stack([grad_cross_keys, grad_cross_values]).reshape(
        2, map_count, TEXT, width_own
    )
    grad_projected = jnp.stack(
        [
            grad_query,
            grad_keys.astype(jnp.bfloat16),
            grad_values.astype(jnp.bfloat16),
            grad_cross_query,
        ]
    ).reshape(4, map_count, token_count, width_own)
    in_part = jnp.einsum(
        "mnc,pmnd->pcd", normed, grad_projected, preferred_element_type=jnp.float32
    )
    grad_normed = own_part(
        jnp.einsum(
            "pmnd,pcd->mnc", grad_projected, in_maps, preferred_element_type=jnp.float32
        ).reshape(map_count, row_count, col_count, C)
    )
    layer_gain_part = jnp.sum(grad_normed * token_scaled, axis=(0, 1, 2))
    layer_bias_part = jnp.sum(grad_normed, axis=(0, 1, 2))
    grad_scaled = grad_normed * layer_gain
    plain_sum, dot_sum = token_total(
        jnp.sum(grad_scaled, axis=3), jnp.sum(grad_scaled * token_scaled, axis=3)
    )
    grad_middle = (
        token_inverse
        * (grad_scaled - plain_sum[..., None] / C - token_scaled * dot_sum[..., None] / C)
        + cotangent
    )
    first_scaled = (source - first_center) * first_inverse
    first_normed = first_scaled * group_gain[0] + group_bias[0]
    first_framed = spread(jax.nn.silu(first_normed).astype(jnp.bfloat16))
    inner = convolve(first_framed, kernels[0])
    lifted = inner * (1.0 + film_scale) + film_shift
    second_scaled = (lifted - second_center) * second_inverse
    second_normed = second_scaled * group_gain[1] + group_bias[1]
    second_framed = spread(jax.nn.silu(second_normed).astype(jnp.bfloat16))
    grad_two = (grad_middle * root_half).astype(jnp.bfloat16)
    second_kernel_grad = kernel_grad(second_framed, grad_two)
    grad_second = own_part(input_grad(grad_two, kernels[1]))
    grad_lifted, gain_two, bias_two, layer_gain_sum, layer_bias_sum = group_backward(
        grad_second * silu_slope(second_normed),
        second_scaled,
        group_gain[1],
        second_inverse,
        pixel_count,
        layer_gain_part[None],
        layer_bias_part[None],
    )
    grad_film = jnp.stack(
        [jnp.sum(grad_lifted * inner, axis=(1, 2)), jnp.sum(grad_lifted, axis=(1, 2))], axis=1
    )
    film_all, text_all = lax.psum((grad_film, text_grads), "wide")
    time_grad = jnp.einsum(
        "mk,msc->ksc", own_features.astype(jnp.float32), film_all, precision=highest
    )
    text_grad = jnp.einsum(
        "mx,msc->xsc", own_pooled.astype(jnp.float32), film_all, precision=highest
    )
    kv_grad = jnp.einsum("mtx,pmtd->pxd", own_text.astype(jnp.float32), text_all, precision=highest)
    grad_one = (grad_lifted * (1.0 + film_scale)).astype(jnp.bfloat16)
    first_kernel_grad = kernel_grad(first_framed, grad_one)
    grad_first = own_part(input_grad(grad_one, kernels[0]))
    empty_rows = jnp.zeros((0, width_own), jnp.float32)
    grad_source, gain_one, bias_one, unused_first, unused_second = group_backward(
        grad_first * silu_slope(first_normed),
        first_scaled,
        group_gain[0],
        first_inverse,
        pixel_count,
        empty_rows,
        empty_rows,
    )
    pixels_grad = grad_source + grad_middle * root_half
    summed = (
        lax.psum_scatter(
            jnp.stack([first_kernel_grad, second_kernel_grad]),
            "wide",
            scatter_dimension=2,
            tiled=True,
        ),
        lax.psum_scatter(in_part, "wide", scatter_dimension=1, tiled=True),
        lax.psum_scatter(out_self_part, "wide", scatter_dimension=1, tiled=True),
        lax.psum_scatter(out_cross_part, "wide", scatter_dimension=1, tiled=True),
    )
    return (
        result,
        pixels_grad,
        summed[0],
        time_grad,
        text_grad,
        jnp.stack([gain_one, gain_two]),
        jnp.stack([bias_one, bias_two]),
        layer_gain_sum[0],
        layer_bias_sum[0],
        summed[1],
        kv_grad,
        summed[2],
        summed[3],
    )


def solution(mesh):
    placed = (
        P(None, "wide", None, "tensor"),
        P(),
        P(),
        P(),
        P(None, None, "wide", "tensor"),
        P("wide", None, "tensor"),
        P("wide", None, "tensor"),
        P(None, "tensor"),
        P(None, "tensor"),
        P("tensor"),
        P("tensor"),
        P(None, "wide", "tensor"),
        P(None, "wide", "tensor"),
        P("tensor", "wide"),
        P("tensor", "wide"),
        P(None, "wide", None, "tensor"),
    )
    return jax.shard_map(
        shards,
        mesh=mesh,
        in_specs=placed,
        out_specs=(
            P(None, "wide", None, "tensor"),
            P(None, "wide", None, "tensor"),
            P(None, None, "wide", "tensor"),
            P("wide", None, "tensor"),
            P("wide", None, "tensor"),
            P(None, "tensor"),
            P(None, "tensor"),
            P("tensor"),
            P("tensor"),
            P(None, "wide", "tensor"),
            P(None, "wide", "tensor"),
            P("tensor", "wide"),
            P("tensor", "wide"),
        ),
        check_vma=False,
    )
```

profile of v0, /device:TPU:0, one launch (start us, length us, event | category | flops | bytes accessed | tf_op | source)
XLA Modules:
  0.0 766.6 jit_solution(6447533652283783071)
XLA Ops:
  12.3 26.0 %all-reduce.7 = (f32[8,32]{1,0:T(8,128)S(1)}, f32[8,32]{1,0:T(8,128)S(1)}, f32[1,2,256]{2,1,0:T(2,128)S(1)}) all-reduce(f32[8,32]{1,0:T(8,128)S(1)} %reshape.898, f32[8,32]{1,0:T(8,128)S(1)} %reshape.897, f32[1,2,256]{2,1,0:T(2,128)S(1)} %fusion.247), channel_id=1, replica_groups=mesh['wide'=8,'tensor'=4] {'wide'}, use_global_device_ids=true, to_apply=%region_4.0 | all-reduce | flops 1024 | bytes 8192 | tf_op jit(solution)/shard_map/psum | solution.py:49
  39.1 16.4 %all_gather.50 = bf16[1,2,128,1024]{3,2,1,0:T(8,128)(2,1)S(1)} all-gather(bf16[1,2,128,256]{3,2,1,0:T(8,128)(2,1)S(1)} %fusion.176), channel_id=1, replica_groups=mesh['wide'=8,'tensor'=4] {'tensor'}, dimensions={3}, use_global_device_ids=true | all-gather | bytes 655360 | tf_op jit(solution)/shard_map/all_gather | solution.py:61
  57.7 3.8 collective-permute-start
  63.4 15.3 %all_gather.59 = bf16[1,2,128,1024]{3,2,1,0:T(8,128)(2,1)S(1)} all-gather(bf16[1,2,128,256]{3,2,1,0:T(8,128)(2,1)S(1)} %convert_element_type.237), channel_id=1, replica_groups=mesh['wide'=8,'tensor'=4] {'tensor'}, dimensions={3}, use_global_device_ids=true | all-gather | bytes 655360 | tf_op jit(solution)/shard_map/all_gather | solution.py:61
  94.7 27.3 %all-reduce.14 = (f32[8,32]{1,0:T(8,128)S(1)}, f32[8,32]{1,0:T(8,128)S(1)}, bf16[2,1,128,256]{3,2,0,1:T(8,128)(2,1)}) all-reduce(f32[8,32]{1,0:T(8,128)S(1)} %reshape.911, f32[8,32]{1,0:T(8,128)S(1)} %reshape.910, f32[2,1,128,256]{3,2,0,1:T(8,128)S(1)} %copy-done.47), channel_id=1, replica_groups=mesh['wide'=8,'tensor'=4] {'wide'}, use_global_device_ids=true, to_apply=%region_11.12 | all-reduce | flops 66048 | bytes 397312 | tf_op jit(solution)/shard_map/psum | solution.py:49
  123.3 16.1 %all-gather = bf16[2,128,1024]{2,1,0:T(8,128)(2,1)S(1)} all-gather(bf16[2,128,256]{2,1,0:T(8,128)(2,1)S(1)} %multiply_convert_fusion.2), channel_id=2, replica_groups=mesh['wide'=8,'tensor'=4] {'tensor'}, dimensions={2}, use_global_device_ids=true | all-gather | bytes 655360 | tf_op jit(solution)/shard_map/all_gather | solution.py:61
  141.5 3.0 collective-permute-start.2
  144.6 10.8 %all_gather.57 = bf16[256,1024]{1,0:T(8,128)(2,1)S(1)} all-gather(bf16[256,128]{1,0:T(8,128)(2,1)S(1)} %copy-done.58), channel_id=1, replica_groups=mesh['wide'=8,'tensor'=4] {'wide'}, dimensions={1}, use_global_device_ids=true | all-gather | bytes 589824 | tf_op jit(solution)/shard_map/all_gather | solution.py:318
  170.4 10.3 %all-reduce.9 = (f32[1,2,128]{2,1,0:T(2,128)S(1)}, f32[1,2,128]{2,1,0:T(2,128)S(1)}) all-reduce(f32[1,2,128]{2,1,0:T(2,128)S(1)} %bitcast.991, f32[1,2,128]{2,1,0:T(2,128)S(1)} %bitcast.990), channel_id=1, replica_groups=mesh['wide'=8,'tensor'=4] {'tensor'}, use_global_device_ids=true, to_apply=%region_16.17 | all-reduce | flops 512 | bytes 4096 | tf_op jit(solution)/shard_map/psum | solution.py:53
  181.5 15.1 %all_gather.53 = bf16[1,2,128,1024]{3,2,1,0:T(8,128)(2,1)S(1)} all-gather(bf16[1,2,128,256]{3,2,1,0:T(8,128)(2,1)S(1)} %add_convert_fusion), channel_id=1, replica_groups=mesh['wide'=8,'tensor'=4] {'tensor'}, dimensions={3}, use_global_device_ids=true | all-gather | bytes 655360 | tf_op jit(solution)/shard_map/all_gather | solution.py:61
  201.7 9.5 %all_gather.58 = bf16[256,1024]{1,0:T(8,128)(2,1)S(1)} all-gather(bf16[256,128]{1,0:T(8,128)(2,1)S(1)} %copy-done.59), channel_id=1, replica_groups=mesh['wide'=8,'tensor'=4] {'wide'}, dimensions={1}, use_global_device_ids=true | all-gather | bytes 589824 | tf_op jit(solution)/shard_map/all_gather | solution.py:319
  216.5 4.5 all-gather.13.cloned.1.call-done
  223.3 23.0 %all-gather.15.cloned.1.call-done = bf16[1,2048,2,128]{3,1,2,0:T(8,128)(2,1)} async-done(((bf16[1,256,2,128]{3,1,2,0:T(8,128)(2,1)}), bf16[1,2048,2,128]{3,1,2,0:T(8,128)(2,1)}) %all-gather.15.cloned.1.call-update) | async-done | bytes 1048592 | tf_op jit(solution)/shard_map/all_gather | solution.py:174
  246.3 8.9 %while.39 = (s32[]{:T(128)}, f32[1,256,2]{1,2,0:T(2,128)S(1)}, f32[1,256,2]{1,2,0:T(2,128)S(1)}, f32[1,256,2,128]{1,3,2,0:T(8,128)}, bf16[2,1,1024,2,128]{4,2,3,...) while((s32[]{:T(128)}, f32[1,256,2]{1,2,0:T(2,128)S(1)}, ...), condition=%wide.region_20.21_spmd.clone, body=%wide.region_17.0_spmd.clone.sunk | while | flops 272829440 | bytes 12222613 | solution.py:197
  255.2 9.9 %all_gather.61 = f32[1,2048,2]{1,2,0:T(2,128)} all-gather(f32[1,256,2]{1,2,0:T(2,128)S(1)} %log_add_fusion), channel_id=1, replica_groups=mesh['wide'=8,'tensor'=4] {'wide'}, dimensions={1}, use_global_device_ids=true | all-gather | bytes 18432 | tf_op jit(solution)/shard_map/all_gather | solution.py:248
  266.8 8.9 %all-gather.1 = f32[2048,2]{0,1:T(2,128)} all-gather(f32[256,2]{0,1:T(2,128)S(1)} %get-tuple-element.480), channel_id=3, replica_groups=mesh['wide'=8,'tensor'=4] {'wide'}, dimensions={0}, use_global_device_ids=true | all-gather | bytes 18432 | tf_op jit(solution)/shard_map/all_gather | solution.py:249
  275.7 12.7 %while.41 = (s32[]{:T(128)}, f32[1,256,2,128]{1,3,2,0:T(8,128)}, f32[1,256,2,128]{1,3,2,0:T(8,128)S(1)}, bf16[2,1,1024,2,128]{4,2,0,3,1:T(8,128)(2,1)}, bf16[1,2...) while((s32[]{:T(128)}, f32[1,256,2,128]{1,3,2,0:T(8,128)}, ...), condition=%wide.region_29.30_spmd.clone, body=%wide.region_28.29_spmd.clone.sunk | while | flops 541392896 | bytes 9889475 | solution.py:288
  290.1 8.6 %while.40 = (s32[]{:T(128)}, f32[1,256,2,128]{1,3,2,0:T(8,128)}, bf16[2,1,1024,2,128]{4,2,3,1,0:T(8,128)(2,1)}, bf16[1,256,2,128]{3,1,2,0:T(8,128)(2,1)S(1)}, f3...) while((s32[]{:T(128)}, f32[1,256,2,128]{1,3,2,0:T(8,128)}, ...), condition=%wide.region_27.28_spmd.clone, body=%wide.region_26.27_spmd.clone.sunk | while | flops 405471232 | bytes 6575794 | solution.py:234
  301.0 3.2 fusion.112
  304.2 21.7 %reduce-scatter.11.cloned.1.call-done = bf16[1,2,128,256]{3,2,1,0:T(8,128)(2,1)} async-done(((bf16[1,2,128,1024]{3,2,1,0:T(8,128)(2,1)}), bf16[1,2,128,256]{3,2,1,0:T(8,128)(2,1)}) %reduce-scatter.11.cloned.1.call-update) | async-done | bytes 131088 | tf_op jit(solution)/shard_map/reduce_scatter | solution.py:65
  327.1 8.7 %all-reduce.8 = (f32[2,128]{1,0:T(2,128)S(1)}, f32[1,2,128]{2,1,0:T(2,128)S(1)}) all-reduce(f32[2,128]{1,0:T(2,128)S(1)} %get-tuple-element.379, f32[1,2,128]{2,1,0:T(2,128)S(1)} %bitcast.981), channel_id=1, replica_groups=mesh['wide'=8,'tensor'=4] {'tensor'}, use_global_device_ids=true, to_apply=%region_35.36 | all-reduce | flops 512 | bytes 4096 | tf_op jit(solution)/shard_map/psum | solution.py:53
  356.3 22.8 %reduce-scatter.13.cloned.1.call-done = bf16[1,2,128,256]{3,2,1,0:T(8,128)(2,1)} async-done(((bf16[1,2,128,1024]{3,2,1,0:T(8,128)(2,1)}), bf16[1,2,128,256]{3,2,1,0:T(8,128)(2,1)}) %reduce-scatter.13.cloned.1.call-update) | async-done | bytes 131088 | tf_op jit(solution)/shard_map/reduce_scatter | solution.py:65
  380.3 11.9 %all-reduce.5 = (f32[2,256]{1,0:T(2,128)S(1)}, f32[2,256]{1,0:T(2,128)S(1)}) all-reduce(f32[2,256]{1,0:T(2,128)S(1)} %pad_maximum_fusion.11, f32[2,256]{1,0:T(2,128)S(1)} %pad_maximum_fusion.12), channel_id=1, replica_groups=mesh['wide'=8,'tensor'=4] {'wide'}, use_global_device_ids=true, to_apply=%region_39.40 | all-reduce | flops 1024 | bytes 8192 | tf_op jit(solution)/shard_map/psum | solution.py:49
  431.8 6.7 pad_maximum_fusion
  438.7 12.4 %all-reduce.13.cloned.1.call-done = f32[2,128,256]{1,2,0:T(8,128)} async-done(((f32[2,128,256]{1,2,0:T(8,128)}), f32[2,128,256]{1,2,0:T(8,128)}) %all-reduce.13.cloned.1.call-update) | async-done | bytes 262160 | tf_op jit(solution)/shard_map/psum | solution.py:497
  453.9 21.0 %reduce-scatter.15.cloned.1.call-done = bf16[1,2,128,256]{3,2,1,0:T(8,128)(2,1)} async-done(((bf16[1,2,128,1024]{3,2,1,0:T(8,128)(2,1)}), bf16[1,2,128,256]{3,2,1,0:T(8,128)(2,1)}) %reduce-scatter.15.cloned.1.call-update) | async-done | bytes 131088 | tf_op jit(solution)/shard_map/reduce_scatter | solution.py:65
  476.0 11.9 %all-reduce.4 = (f32[1,256]{1,0:T(1,128)S(1)}, f32[1,256]{1,0:T(1,128)S(1)}, f32[2,256]{1,0:T(2,128)S(1)}) all-reduce(f32[1,256]{1,0:T(1,128)S(1)} %bitcast.988, f32[1,256]{1,0:T(1,128)S(1)} %bitcast.989, f32[2,256]{1,0:T(2,128)S(1)} %maximum_bitcast_fusion.1), channel_id=1, replica_groups=mesh['wide'=8,'tensor'=4] {'wide'}, use_global_device_ids=true, to_apply=%region_47.48 | all-reduce | flops 1024 | bytes 8192 | tf_op jit(solution)/shard_map/psum | solution.py:49
  493.0 4.0 reduce-scatter.9.cloned.1.call-done
  499.1 51.4 %reduce-scatter.19.cloned.1.call-done = f32[4,128,256]{1,2,0:T(8,128)} async-done(((f32[4,1024,256]{1,2,0:T(8,128)}), f32[4,128,256]{1,2,0:T(8,128)}) %reduce-scatter.19.cloned.1.call-update) | async-done | bytes 524304 | tf_op jit(solution)/shard_map/reduce_scatter | solution.py:526
  552.5 37.8 %reduce-scatter.23.cloned.1.call-done = f32[256,128]{1,0:T(8,128)} async-done(((f32[256,1024]{1,0:T(8,128)}), f32[256,128]{1,0:T(8,128)}) %reduce-scatter.23.cloned.1.call-update) | async-done | bytes 131088 | tf_op jit(solution)/shard_map/reduce_scatter | solution.py:528
  590.3 39.6 %reduce-scatter.21.cloned.1.call-done = f32[256,128]{1,0:T(8,128)} async-done(((f32[256,1024]{1,0:T(8,128)}), f32[256,128]{1,0:T(8,128)}) %reduce-scatter.21.cloned.1.call-update) | async-done | bytes 131088 | tf_op jit(solution)/shard_map/reduce_scatter | solution.py:527
  629.9 130.2 %reduce-scatter.17.cloned.1.call-done = f32[2,9,128,256]{3,2,1,0:T(8,128)} async-done(((f32[2,9,1024,256]{3,2,1,0:T(8,128)}), f32[2,9,128,256]{3,2,1,0:T(8,128)}) %reduce-scatter.17.cloned.1.call-update) | async-done | bytes 2359312 | tf_op jit(solution)/shard_map/reduce_scatter | solution.py:520
  (491 shorter events, 166.2 us)
Async XLA Ops:
  7.2 74.5 %all-gather.9.cloned.1.call-start = ((), (), s32[]{:S(2)}) async-start(), calls=%async_computation.8 | async-start | bytes 10616832 | tf_op jit(solution)/shard_map/all_gather | solution.py:316
  8.0 188.6 %all-gather.11.cloned.1.call-start = ((), (), s32[]{:S(2)}) async-start(), calls=%async_computation.9 | async-start | bytes 2359296 | tf_op jit(solution)/shard_map/all_gather | solution.py:317
  9.8 53.5 %copy-start.22 = (f32[1,2,128,256]{3,2,1,0:T(8,128)S(1)}, f32[1,2,128,256]{3,2,1,0:T(8,128)}, u32[]{:S(2)}) copy-start(f32[1,2,128,256]{3,2,1,0:T(8,128)} %param.37) | copy-start | bytes 786436
  12.1 66.5 %copy-start.49 = (bf16[2,512,256]{2,1,0:T(8,128)(2,1)S(1)}, bf16[2,512,256]{2,1,0:T(8,128)(2,1)}, u32[]{:S(2)}) copy-start(bf16[2,512,256]{2,1,0:T(8,128)(2,1)} %param.34) | copy-start | bytes 1572868
  38.9 83.7 %copy-start.88 = (f32[1,256]{1,0:T(1,128)}, f32[1,256]{1,0:T(1,128)S(1)}, u32[]{:S(2)}) copy-start(f32[1,256]{1,0:T(1,128)S(1)} %get-tuple-element.499) | copy-start | bytes 3076
  39.0 83.6 %copy-start.76 = (f32[1,256]{1,0:T(1,128)}, f32[1,256]{1,0:T(1,128)S(1)}, u32[]{:S(2)}) copy-start(f32[1,256]{1,0:T(1,128)S(1)} %get-tuple-element.497) | copy-start | bytes 3076
  56.4 23.2 %collective-permute-start.1 = (bf16[1,1,128,1024]{3,2,1,0:T(8,128)(2,1)}, bf16[1,1,128,1024]{3,2,1,0:T(8,128)(2,1)S(1)}, u32[]{:S(2)}, u32[]{:S(2)}) collective-permute-start(bf16[1,1,128,1024]{3,2,1,0:T(8,128)(2,1)} %get-tuple-element.479), channel_id=1, source_target_pairs={{4,0},{8,4},{12,8},{16,12},{20,16},{24,20},{28,24},{5,1},{9,5},{13... | collective-permute-start | bytes 786440 | tf_op jit(solution)/shard_map/ppermute | solution.py:29
  57.7 22.6 %collective-permute-start = (bf16[1,1,128,1024]{3,2,1,0:T(8,128)(2,1)}, bf16[1,1,128,1024]{3,2,1,0:T(8,128)(2,1)}, u32[]{:S(2)}, u32[]{:S(2)}) collective-permute-start(bf16[1,1,128,1024]{3,2,1,0:T(8,128)(2,1)} %get-tuple-element.478), channel_id=1, source_target_pairs={{0,4},{4,8},{8,12},{12,16},{16,20},{20,24},{24,28},{1,5},{5,9},{9,... | collective-permute-start | bytes 786440 | tf_op jit(solution)/shard_map/ppermute | solution.py:27
  63.3 148.3 %all-gather.19.cloned.1.call-start = ((), (), s32[]{:S(2)}) async-start(), calls=%async_computation.14 | async-start | bytes 1179648 | tf_op jit(solution)/shard_map/all_gather | solution.py:247
  78.6 132.6 %copy-start.6 = (bf16[1,2,128,1024]{3,2,1,0:T(8,128)(2,1)}, bf16[1,2,128,1024]{3,2,1,0:T(8,128)(2,1)S(1)}, u32[]{:S(2)}) copy-start(bf16[1,2,128,1024]{3,2,1,0:T(8,128)(2,1)S(1)} %all_gather.59) | copy-start | bytes 1572868
  93.1 51.4 %copy-start.58 = (bf16[256,128]{1,0:T(8,128)(2,1)S(1)}, bf16[256,128]{1,0:T(8,128)(2,1)}, u32[]{:S(2)}) copy-start(bf16[256,128]{1,0:T(8,128)(2,1)} %param.35) | copy-start | bytes 196612
  94.5 63.0 %copy-start.25 = (f32[2,128,256]{2,1,0:T(8,128)}, f32[2,128,256]{2,1,0:T(8,128)S(1)}, u32[]{:S(2)}) copy-start(f32[2,128,256]{2,1,0:T(8,128)S(1)} %get-tuple-element.502) | copy-start | bytes 786436
  140.2 17.0 %collective-permute-start.3 = (bf16[1,1,128,1024]{3,2,1,0:T(8,128)(2,1)}, bf16[1,1,128,1024]{3,2,1,0:T(8,128)(2,1)S(1)}, u32[]{:S(2)}, u32[]{:S(2)}) collective-permute-start(bf16[1,1,128,1024]{3,2,1,0:T(8,128)(2,1)} %get-tuple-element.477), channel_id=1, source_target_pairs={{4,0},{8,4},{12,8},{16,12},{20,16},{24,20},{28,24},{5,1},{9,5},{13... | collective-permute-start | bytes 786440 | tf_op jit(solution)/shard_map/ppermute | solution.py:29
  141.5 15.8 %collective-permute-start.2 = (bf16[1,1,128,1024]{3,2,1,0:T(8,128)(2,1)S(1)}, bf16[1,1,128,1024]{3,2,1,0:T(8,128)(2,1)S(1)}, u32[]{:S(2)}, u32[]{:S(2)}) collective-permute-start(bf16[1,1,128,1024]{3,2,1,0:T(8,128)(2,1)S(1)} %get-tuple-element.476), channel_id=1, source_target_pairs={{0,4},{4,8},{8,12},{12,16},{16,20},{20,24},{24,28},{1,5},{5,9},{9,... | collective-permute-start | bytes 786440 | tf_op jit(solution)/shard_map/ppermute | solution.py:27
  157.2 63.8 %all-gather.13.cloned.1.call-start = ((), (), s32[]{:S(2)}) async-start(), calls=%async_computation.10 | async-start | bytes 1179648 | tf_op jit(solution)/shard_map/all_gather | solution.py:173
  200.0 46.3 %all-gather.15.cloned.1.call-start = ((), (), s32[]{:S(2)}) async-start(), calls=%async_computation.11 | async-start | bytes 1179648 | tf_op jit(solution)/shard_map/all_gather | solution.py:174
  200.8 74.9 %all-gather.17.cloned.1.call-start = ((), (), s32[]{:S(2)}) async-start(), calls=%async_computation.13 | async-start | bytes 1179648 | tf_op jit(solution)/shard_map/all_gather | solution.py:246
  216.3 109.6 %reduce-scatter.11.cloned.1.call-start = ((), (), s32[]{:S(2)}) async-start(), calls=%async_computation.15 | async-start | bytes 655360 | tf_op jit(solution)/shard_map/reduce_scatter | solution.py:65
  304.2 75.0 %reduce-scatter.13.cloned.1.call-start = ((), (), s32[]{:S(2)}) async-start(), calls=%async_computation.16 | async-start | bytes 655360 | tf_op jit(solution)/shard_map/reduce_scatter | solution.py:65
  337.0 4.3 collective-permute-start.5
  338.3 3.9 collective-permute-start.4
  355.8 95.2 %all-reduce.13.cloned.1.call-start = ((), (), s32[]{:S(2)}) async-start(), calls=%async_computation.20 | async-start | bytes 524288 | tf_op jit(solution)/shard_map/psum | solution.py:497
  394.2 5.4 collective-permute-start.7
  395.5 4.1 collective-permute-start.6
  399.3 75.6 %reduce-scatter.15.cloned.1.call-start = ((), (), s32[]{:S(2)}) async-start(), calls=%async_computation.17 | async-start | bytes 655360 | tf_op jit(solution)/shard_map/reduce_scatter | solution.py:65
  413.1 84.0 %reduce-scatter.9.cloned.1.call-start = ((), (), s32[]{:S(2)}) async-start(), calls=%async_computation.12 | async-start | bytes 655360 | tf_op jit(solution)/shard_map/reduce_scatter | solution.py:65
  415.2 135.3 %reduce-scatter.19.cloned.1.call-start = ((), (), s32[]{:S(2)}) async-start(), calls=%async_computation.19 | async-start | bytes 4718592 | tf_op jit(solution)/shard_map/reduce_scatter | solution.py:526
  418.1 172.2 %reduce-scatter.23.cloned.1.call-start = ((), (), s32[]{:S(2)}) async-start(), calls=%async_computation.22 | async-start | bytes 1179648 | tf_op jit(solution)/shard_map/reduce_scatter | solution.py:528
  420.5 209.4 %reduce-scatter.21.cloned.1.call-start = ((), (), s32[]{:S(2)}) async-start(), calls=%async_computation.21 | async-start | bytes 1179648 | tf_op jit(solution)/shard_map/reduce_scatter | solution.py:527
  422.9 337.2 %reduce-scatter.17.cloned.1.call-start = ((), (), s32[]{:S(2)}) async-start(), calls=%async_computation.18 | async-start | bytes 21233664 | tf_op jit(solution)/shard_map/reduce_scatter | solution.py:520
  438.7 51.2 %copy-start.109 = (f32[128]{0:T(128)S(1)}, f32[128]{0:T(128)}, u32[]{:S(2)}) copy-start(f32[128]{0:T(128)} %get-tuple-element.464) | copy-start | bytes 1540
  438.7 52.1 %copy-start.95 = (f32[512]{0:T(512)S(1)}, f32[512]{0:T(512)}, u32[]{:S(2)}) copy-start(f32[512]{0:T(512)} %get-tuple-element.462) | copy-start | bytes 6148
  (108 other events, 1723.5 us)
Sparse Core Ops, SparseCore 0:
  10.0 66.9 all-gather.8
  79.4 29.4 all-gather.10
  157.3 22.1 all-gather.18
  200.1 20.8 all-gather.12
  222.8 23.4 all-gather.14
  248.6 23.5 all-gather.16
  304.3 21.5 reduce-scatter.10
  355.9 23.1 reduce-scatter.12
  399.4 51.5 all-reduce.12
  453.8 21.0 reduce-scatter.14
  477.3 19.7 reduce-scatter.8
  500.6 49.8 reduce-scatter.18
  554.2 36.0 reduce-scatter.22
  593.9 35.9 reduce-scatter.20
  634.0 126.0 reduce-scatter.16
where the time goes:
time: 770 us; the launch traced here: 767 us
  waiting for transfers between devices  370 us (48%)
  blocking collectives  198 us (26%)
  matrix products  107 us (14%)
  other arithmetic  31.2 us (4%)
  local copies, waits for them, and re-layouts  24.3 us (3%)
  starting transfers between devices  19 us (2%)
  between operations  17.1 us (2%)
    reduce_scatter x1, waiting for transfers between devices, shards(): lax.psum_scatter(jnp.stack([first_kernel_grad, second_kernel_grad]), 'wid...  130 us
    psum x4, blocking collectives, wide_total(): return lax.psum((first, second), 'wide')  77.1 us
    reduce_scatter x4, waiting for transfers between devices, own_part(): lax.psum_scatter(values.astype(jnp.bfloat16), 'tensor', scatter_dimension...  69.5 us
    all_gather x4, blocking collectives, full_channels(): return lax.all_gather(values, 'tensor', axis=3, tiled=True)  62.9 us
    reduce_scatter x1, waiting for transfers between devices, shards(): lax.psum_scatter(in_part, 'wide', scatter_dimension=1, tiled=True)  51.4 us
    reduce_scatter x1, waiting for transfers between devices, shards(): lax.psum_scatter(out_self_part, 'wide', scatter_dimension=1, tiled=True)  39.6 us
    reduce_scatter x1, waiting for transfers between devices, shards(): lax.psum_scatter(out_cross_part, 'wide', scatter_dimension=1, tiled=True)  37.8 us
    dot_general x18, matrix products, input_grad(): jnp.einsum('mrwd,cd->mrwc', window, kernel[position], preferred_element_t...  26.5 us
  transfers between devices with their start and end apart: 23, of which 12 were waited for; matrix products, arithmetic and copies ran while one was open for 14% of the time, Pallas kernels for 0%

commit v1 on v0

--- a/solution.py
+++ b/solution.py
@@ -45,12 +45,27 @@
     return logistic * (1.0 + values * (1.0 - logistic))
 
 
+def flipped(values, axis, mask):
+    count = lax.axis_size(axis)
+    return lax.ppermute(values, axis, [(i, i ^ mask) for i in range(count)])
+
+
+def total(values, axis):
+    mask = 1
+    while mask < lax.axis_size(axis):
+        values = values + flipped(values, axis, mask)
+        mask *= 2
+    return values
+
+
 def wide_total(first, second):
-    return lax.psum((first, second), "wide")
+    both = total(jnp.stack([first, second]), "wide")
+    return both[0], both[1]
 
 
 def token_total(first, second):
-    return lax.psum((first, second), "tensor")
+    both = total(jnp.stack([first, second]), "tensor")
+    return both[0], both[1]
 
 
 def rows_of(values):
@@ -117,7 +132,11 @@
     return summed
 
 
-def kernel_grad(framed, grad_low):
+def kernel_grad(own_framed, own_grad):
+    own = own_framed[:, 1:-1, 1:-1, :]
+    swapped = lax.all_to_all(own, "wide", split_axis=3, concat_axis=1, tiled=True)
+    framed = jnp.pad(swapped, ((0, 0), (1, 1), (1, 1), (0, 0)))
+    grad_low = lax.all_gather(own_grad, "wide", axis=1, tiled=True)
     row_count = grad_low.shape[1]
     col_count = grad_low.shape[2]
     return jnp.stack(
@@ -313,7 +332,10 @@
     pixel_count = row_count * lax.axis_size("wide") * col_count * (C // GROUPS)
     score_scale = HEAD_DIM ** (-0.5)
     gathered = (
-        lax.all_gather(conv_weights, "wide", axis=2, tiled=True),
+        (
+            lax.all_gather(conv_weights[0], "wide", axis=1, tiled=True),
+            lax.all_gather(conv_weights[1], "wide", axis=1, tiled=True),
+        ),
         lax.all_gather(attn_in, "wide", axis=1, tiled=True),
         lax.all_gather(out_self, "wide", axis=1, tiled=True),
         lax.all_gather(out_cross, "wide", axis=1, tiled=True),
@@ -335,8 +357,8 @@
         "mk,ksc->msc", own_features, film_time, preferred_element_type=jnp.float32
     ) + jnp.einsum("mk,ksc->msc", own_pooled, film_text, preferred_element_type=jnp.float32)
     text_term = jnp.einsum("mtx,pxd->pmtd", own_text, text_kv, preferred_element_type=jnp.float32)
-    film, text_total = lax.psum((film_term, text_term), "wide")
-    text_proj = text_total.astype(jnp.bfloat16)
+    film = total(film_term, "wide")
+    text_proj = lax.psum(text_term.astype(jnp.bfloat16), "wide")
     film_scale = film[:, 0][:, None, None, :]
     film_shift = film[:, 1][:, None, None, :]
     source = pixels.astype(jnp.float32)
@@ -385,13 +407,6 @@
         "mnh,hc->mnc", attended_low, self_out, preferred_element_type=jnp.float32
     ) + jnp.einsum("mnh,hc->mnc", crossed_low, cross_out, preferred_element_type=jnp.float32)
     result = middle + own_part(mixed.reshape(map_count, row_count, col_count, C))
-    regathered = (
-        lax.all_gather(conv_weights, "wide", axis=2, tiled=True),
-        lax.all_gather(attn_in, "wide", axis=1, tiled=True),
-        lax.all_gather(out_self, "wide", axis=1, tiled=True),
-        lax.all_gather(out_cross, "wide", axis=1, tiled=True),
-    )
-    kernels, in_maps, self_out, cross_out = regathered
     grad_full = full_channels(cotangent.astype(jnp.bfloat16)).reshape(map_count, token_count, C)
     out_self_part = jnp.einsum(
         "mnh,mnc->hc", attended_low, grad_full, preferred_element_type=jnp.float32
@@ -471,14 +486,6 @@
         * (grad_scaled - plain_sum[..., None] / C - token_scaled * dot_sum[..., None] / C)
         + cotangent
     )
-    first_scaled = (source - first_center) * first_inverse
-    first_normed = first_scaled * group_gain[0] + group_bias[0]
-    first_framed = spread(jax.nn.silu(first_normed).astype(jnp.bfloat16))
-    inner = convolve(first_framed, kernels[0])
-    lifted = inner * (1.0 + film_scale) + film_shift
-    second_scaled = (lifted - second_center) * second_inverse
-    second_normed = second_scaled * group_gain[1] + group_bias[1]
-    second_framed = spread(jax.nn.silu(second_normed).astype(jnp.bfloat16))
     grad_two = (grad_middle * root_half).astype(jnp.bfloat16)
     second_kernel_grad = kernel_grad(second_framed, grad_two)
     grad_second = own_part(input_grad(grad_two, kernels[1]))
@@ -494,7 +501,8 @@
     grad_film = jnp.stack(
         [jnp.sum(grad_lifted * inner, axis=(1, 2)), jnp.sum(grad_lifted, axis=(1, 2))], axis=1
     )
-    film_all, text_all = lax.psum((grad_film, text_grads), "wide")
+    film_all = total(grad_film, "wide")
+    text_all = lax.psum(text_grads.astype(jnp.bfloat16), "wide").astype(jnp.float32)
     time_grad = jnp.einsum(
         "mk,msc->ksc", own_features.astype(jnp.float32), film_all, precision=highest
     )
@@ -516,31 +524,31 @@
         empty_rows,
     )
     pixels_grad = grad_source + grad_middle * root_half
-    summed = (
+    parts = (
         lax.psum_scatter(
-            jnp.stack([first_kernel_grad, second_kernel_grad]),
+            in_part.astype(jnp.bfloat16), "wide", scatter_dimension=1, tiled=True
+        ).astype(jnp.float32),
+        lax.psum_scatter(
+            jnp.concatenate([out_self_part, out_cross_part]).astype(jnp.bfloat16),
             "wide",
-            scatter_dimension=2,
+            scatter_dimension=1,
             tiled=True,
-        ),
-        lax.psum_scatter(in_part, "wide", scatter_dimension=1, tiled=True),
-        lax.psum_scatter(out_self_part, "wide", scatter_dimension=1, tiled=True),
-        lax.psum_scatter(out_cross_part, "wide", scatter_dimension=1, tiled=True),
+        ).astype(jnp.float32),
     )
     return (
         result,
         pixels_grad,
-        summed[0],
+        jnp.stack([first_kernel_grad, second_kernel_grad]),
         time_grad,
         text_grad,
         jnp.stack([gain_one, gain_two]),
         jnp.stack([bias_one, bias_two]),
         layer_gain_sum[0],
         layer_bias_sum[0],
-        summed[1],
+        parts[0],
         kv_grad,
-        summed[2],
-        summed[3],
+        parts[1][:width_own],
+        parts[1][width_own:],
     )
 
 

time: 770 us -> 647 us (0.84)
  blocking collectives: 198 us -> 121 us
  waiting for transfers between devices: 370 us -> 299 us
  starting transfers between devices: 19 us -> 39.8 us
  matrix products: 107 us -> 93.7 us
  local copies, waits for them, and re-layouts: 24.3 us -> 35.3 us
    reduce_scatter x4 -> x0, waiting for transfers between devices: 259 us -> none  [the longest x1 130 us: shards(): lax.psum_scatter(jnp.stack([first_kernel_grad, second_kernel_grad]), 'wid...]
    psum x6 -> x0, blocking collectives: 96.1 us -> none  [the longest x4 77.1 us: wide_total(): return lax.psum((first, second), 'wide')]
    unnamed x15 -> x19, waiting for transfers between devices: 0.91 us -> 60.3 us
    ppermute x0 -> x22, waiting for transfers between devices: none -> 42.5 us  [flipped(): return lax.ppermute(values, axis, [(i, i ^ mask) for i in range(count)])]
    all_gather x1 -> x4, waiting for transfers between devices: 0.02 us -> 35.9 us  [the longest x2 35.9 us: kernel_grad(): grad_low = lax.all_gather(own_grad, 'wide', axis=1, tiled=True)]
    ppermute x0 -> x22, starting transfers between devices: none -> 23.8 us  [flipped(): return lax.ppermute(values, axis, [(i, i ^ mask) for i in range(count)])]
    all_gather x1, waiting for transfers between devices: 0.02 us -> 23.8 us  [key_grads(): lax.all_gather(grad_wide, 'wide', axis=1, tiled=True)]
    all_to_all x0 -> x1, blocking collectives: none -> 16.3 us  [kernel_grad(): lax.all_to_all(own, 'wide', split_axis=3, concat_axis=1, tiled=True)]
  transfers between devices with their start and end apart: 23 -> 48, of which waited for: 12 -> 34; matrix products, arithmetic and copies ran while one was open for 14% -> 18% of each run, Pallas kernels for 0% -> 0%
where the time goes in v1:
time: 647 us; the launch traced here: 638 us
  waiting for transfers between devices  299 us (46%)
  blocking collectives  121 us (19%)
  matrix products  93.7 us (14%)
  starting transfers between devices  39.8 us (6%)
  local copies, waits for them, and re-layouts  35.3 us (5%)
  other arithmetic  31 us (5%)
  between operations  17.7 us (3%)
    reduce_scatter x4, waiting for transfers between devices, own_part(): lax.psum_scatter(values.astype(jnp.bfloat16), 'tensor', scatter_dimension...  72.5 us
    all_gather x4, blocking collectives, full_channels(): return lax.all_gather(values, 'tensor', axis=3, tiled=True)  63.8 us
    unnamed x19, waiting for transfers between devices  60.3 us
    ppermute x22, waiting for transfers between devices, flipped(): return lax.ppermute(values, axis, [(i, i ^ mask) for i in range(count)])  42.5 us
    all_gather x2, waiting for transfers between devices, kernel_grad(): grad_low = lax.all_gather(own_grad, 'wide', axis=1, tiled=True)  35.9 us
    ppermute x22, starting transfers between devices, flipped(): return lax.ppermute(values, axis, [(i, i ^ mask) for i in range(count)])  23.8 us
    all_gather x1, waiting for transfers between devices, key_grads(): lax.all_gather(grad_wide, 'wide', axis=1, tiled=True)  23.8 us
    all_gather x1, waiting for transfers between devices, attend_forward(): lax.all_gather(values, 'wide', axis=1, tiled=True)  23.3 us
  transfers between devices with their start and end apart: 48, of which 34 were waited for; matrix products, arithmetic and copies ran while one was open for 18% of the time, Pallas kernels for 0%

profile of v1, /device:TPU:0, one launch (start us, length us, event | category | flops | bytes accessed | tf_op | source)
XLA Modules:
  0.0 637.7 jit_solution(18150406222388321914)
XLA Ops:
  24.1 16.4 %all_gather.53 = bf16[1,2,128,1024]{3,2,1,0:T(8,128)(2,1)S(1)} all-gather(bf16[1,2,128,256]{3,2,1,0:T(8,128)(2,1)S(1)} %fusion.236), channel_id=1, replica_groups=mesh['wide'=8,'tensor'=4] {'tensor'}, dimensions={3}, use_global_device_ids=true | all-gather | bytes 655360 | tf_op jit(solution)/shard_map/all_gather | solution.py:76
  48.9 7.2 %collective-permute-done.6 = f32[1,2,256]{2,1,0:T(2,128)S(1)} collective-permute-done((f32[1,2,256]{2,1,0:T(2,128)S(1)}, f32[1,2,256]{2,1,0:T(2,128)S(1)}, u32[]{:S(2)}, u32[]{:S(2)}) %collective-permute-start.6) | collective-permute-done | bytes 2080 | tf_op jit(solution)/shard_map/ppermute | solution.py:50
  56.1 3.6 collective-permute-done.7
  69.3 3.6 collective-permute-done.9
  77.9 15.2 %all-gather.1 = bf16[2,128,1024]{2,1,0:T(8,128)(2,1)S(1)} all-gather(bf16[2,128,256]{2,1,0:T(8,128)(2,1)S(1)} %multiply_convert_fusion.2), channel_id=3, replica_groups=mesh['wide'=8,'tensor'=4] {'tensor'}, dimensions={2}, use_global_device_ids=true | all-gather | bytes 655360 | tf_op jit(solution)/shard_map/all_gather | solution.py:76
  95.8 13.5 %all_gather.61 = bf16[256,1024]{1,0:T(8,128)(2,1)S(1)} all-gather(bf16[256,128]{1,0:T(8,128)(2,1)S(1)} %copy-done.53), channel_id=1, replica_groups=mesh['wide'=8,'tensor'=4] {'wide'}, dimensions={1}, use_global_device_ids=true | all-gather | bytes 589824 | tf_op jit(solution)/shard_map/all_gather | solution.py:340
  109.3 16.9 %all_gather.63 = bf16[1,2,128,1024]{3,2,1,0:T(8,128)(2,1)S(1)} all-gather(bf16[1,2,128,256]{3,2,1,0:T(8,128)(2,1)S(1)} %convert_element_type.271), channel_id=1, replica_groups=mesh['wide'=8,'tensor'=4] {'tensor'}, dimensions={3}, use_global_device_ids=true | all-gather | bytes 655360 | tf_op jit(solution)/shard_map/all_gather | solution.py:76
  144.2 15.3 %all_gather.57 = bf16[1,2,128,1024]{3,2,1,0:T(8,128)(2,1)S(1)} all-gather(bf16[1,2,128,256]{3,2,1,0:T(8,128)(2,1)S(1)} %add_convert_fusion), channel_id=1, replica_groups=mesh['wide'=8,'tensor'=4] {'tensor'}, dimensions={3}, use_global_device_ids=true | all-gather | bytes 655360 | tf_op jit(solution)/shard_map/all_gather | solution.py:76
  165.3 8.9 %all_gather.62 = bf16[256,1024]{1,0:T(8,128)(2,1)S(1)} all-gather(bf16[256,128]{1,0:T(8,128)(2,1)S(1)} %copy-done.54), channel_id=1, replica_groups=mesh['wide'=8,'tensor'=4] {'wide'}, dimensions={1}, use_global_device_ids=true | all-gather | bytes 589824 | tf_op jit(solution)/shard_map/all_gather | solution.py:341
  175.4 8.9 %all-reduce.9.cloned.1.call-done = bf16[2,1,128,256]{3,2,0,1:T(8,128)(2,1)} async-done(((bf16[2,1,128,256]{3,2,0,1:T(8,128)(2,1)}), bf16[2,1,128,256]{3,2,0,1:T(8,128)(2,1)}) %all-reduce.9.cloned.1.call-update) | async-done | bytes 131088 | tf_op jit(solution)/shard_map/psum | solution.py:361
  185.3 23.8 %all-gather.22.cloned.1.call-done = bf16[1,2048,2,128]{1,3,2,0:T(8,128)(2,1)} async-done(((bf16[1,256,2,128]{1,3,2,0:T(8,128)(2,1)}), bf16[1,2048,2,128]{1,3,2,0:T(8,128)(2,1)}) %all-gather.22.cloned.1.call-update) | async-done | bytes 1048592 | tf_op jit(solution)/shard_map/all_gather | solution.py:266
  214.7 19.9 %all-gather.16.cloned.1.call-done = bf16[1,2048,2,128]{3,1,2,0:T(8,128)(2,1)} async-done(((bf16[1,256,2,128]{3,1,2,0:T(8,128)(2,1)}), bf16[1,2048,2,128]{3,1,2,0:T(8,128)(2,1)}) %all-gather.16.cloned.1.call-update) | async-done | bytes 1048592 | tf_op jit(solution)/shard_map/all_gather | solution.py:192
  236.9 23.3 %all-gather.18.cloned.1.call-done = bf16[1,2048,2,128]{3,1,2,0:T(8,128)(2,1)} async-done(((bf16[1,256,2,128]{3,1,2,0:T(8,128)(2,1)}), bf16[1,2048,2,128]{3,1,2,0:T(8,128)(2,1)}) %all-gather.18.cloned.1.call-update) | async-done | bytes 1048592 | tf_op jit(solution)/shard_map/all_gather | solution.py:193
  260.2 8.5 %while.39 = (s32[]{:T(128)}, f32[1,256,2]{1,2,0:T(2,128)S(1)}, f32[1,256,2]{1,2,0:T(2,128)S(1)}, f32[1,256,2,128]{1,3,2,0:T(8,128)}, bf16[2,1,1024,2,128]{4,2,3,...) while((s32[]{:T(128)}, f32[1,256,2]{1,2,0:T(2,128)S(1)}, ...), condition=%wide.region_13.14_spmd.clone, body=%wide.region_10.0_spmd.clone.sunk | while | flops 272829440 | bytes 8029289 | solution.py:216
  270.4 8.5 %while.40 = (s32[]{:T(128)}, f32[1,256,2,128]{1,3,2,0:T(8,128)}, bf16[2,1,1024,2,128]{4,2,3,1,0:T(8,128)(2,1)}, bf16[1,256,2,128]{3,1,2,0:T(8,128)(2,1)S(1)}, f3...) while((s32[]{:T(128)}, f32[1,256,2,128]{1,3,2,0:T(8,128)}, ...), condition=%wide.region_20.21_spmd.clone, body=%wide.region_19.20_spmd.clone.sunk | while | flops 405471232 | bytes 6559343 | solution.py:253
  280.5 9.8 %all-gather.3 = f32[2048,2]{0,1:T(2,128)} all-gather(f32[256,2]{0,1:T(2,128)S(1)} %bitcast.1133), channel_id=5, replica_groups=mesh['wide'=8,'tensor'=4] {'wide'}, dimensions={0}, use_global_device_ids=true | all-gather | bytes 18432 | tf_op jit(solution)/shard_map/all_gather | solution.py:268
  290.3 8.9 %all_gather.65 = f32[1,2048,2]{1,2,0:T(2,128)} all-gather(f32[1,256,2]{1,2,0:T(2,128)S(1)} %get-tuple-element.882), channel_id=1, replica_groups=mesh['wide'=8,'tensor'=4] {'wide'}, dimensions={1}, use_global_device_ids=true | all-gather | bytes 18432 | tf_op jit(solution)/shard_map/all_gather | solution.py:267
  299.2 12.7 %while.41 = (s32[]{:T(128)}, f32[1,256,2,128]{1,3,2,0:T(8,128)}, f32[1,256,2,128]{1,3,2,0:T(8,128)S(1)}, bf16[2,1,1024,2,128]{4,2,0,3,1:T(8,128)(2,1)}, bf16[1,2...) while((s32[]{:T(128)}, f32[1,256,2,128]{1,3,2,0:T(8,128)}, ...), condition=%wide.region_22.23_spmd.clone, body=%wide.region_21.22_spmd.clone.sunk | while | flops 541392896 | bytes 10414288 | solution.py:307
  318.2 21.9 %reduce-scatter.13.cloned.1.call-done = bf16[1,2,128,256]{3,2,1,0:T(8,128)(2,1)} async-done(((bf16[1,2,128,1024]{3,2,1,0:T(8,128)(2,1)}), bf16[1,2,128,256]{3,2,1,0:T(8,128)(2,1)}) %reduce-scatter.13.cloned.1.call-update) | async-done | bytes 131088 | tf_op jit(solution)/shard_map/reduce_scatter | solution.py:80
  341.8 3.6 collective-permute-done.15
  346.1 3.8 collective-permute-done.16
  354.0 3.4 collective-permute-done.18
  369.4 17.9 %reduce-scatter.15.cloned.1.call-done = bf16[1,2,128,256]{3,2,1,0:T(8,128)(2,1)} async-done(((bf16[1,2,128,1024]{3,2,1,0:T(8,128)(2,1)}), bf16[1,2,128,256]{3,2,1,0:T(8,128)(2,1)}) %reduce-scatter.15.cloned.1.call-update) | async-done | bytes 131088 | tf_op jit(solution)/shard_map/reduce_scatter | solution.py:80
  423.3 16.3 %all_to_all.36 = bf16[1,2,128,1024]{2,1,0,3:T(2,128)(2,1)S(1)} all-to-all(bf16[1,2,128,1024]{2,1,0,3:T(2,128)(2,1)S(1)} %copy.223), channel_id=1, replica_groups=mesh['wide'=8,'tensor'=4] {'wide'}, dimensions={3} | all-to-all | bytes 1048576 | tf_op jit(solution)/shard_map/all_to_all | solution.py:137
  440.8 4.3 all-to-all-start.1
  449.9 4.9 all-to-all-done.1
  456.0 25.1 %reduce-scatter.21.cloned.1.call-done = bf16[128,512]{1,0:T(8,128)(2,1)} async-done(((bf16[1024,512]{1,0:T(8,128)(2,1)}), bf16[128,512]{1,0:T(8,128)(2,1)}) %reduce-scatter.21.cloned.1.call-update) | async-done | bytes 131088
  492.6 14.4 %all-gather.26.cloned.1.call-done = bf16[1,16,128,256]{3,2,0,1:T(8,128)(2,1)} async-done(((bf16[1,2,128,256]{3,2,0,1:T(8,128)(2,1)}), bf16[1,16,128,256]{3,2,0,1:T(8,128)(2,1)}) %all-gather.26.cloned.1.call-update) | async-done | bytes 1048592 | tf_op jit(solution)/shard_map/all_gather | solution.py:139
  515.6 15.8 %reduce-scatter.17.cloned.1.call-done = bf16[1,2,128,256]{3,2,1,0:T(8,128)(2,1)} async-done(((bf16[1,2,128,1024]{3,2,1,0:T(8,128)(2,1)}), bf16[1,2,128,256]{3,2,1,0:T(8,128)(2,1)}) %reduce-scatter.17.cloned.1.call-update) | async-done | bytes 131088 | tf_op jit(solution)/shard_map/reduce_scatter | solution.py:80
  540.4 34.2 %reduce-scatter.19.cloned.1.call-done = bf16[128,1024]{1,0:T(8,128)(2,1)} async-done(((bf16[1024,1024]{1,0:T(8,128)(2,1)}), bf16[128,1024]{1,0:T(8,128)(2,1)}) %reduce-scatter.19.cloned.1.call-update) | async-done | bytes 262160
  581.6 16.9 %reduce-scatter.11.cloned.1.call-done = bf16[1,2,128,256]{3,2,1,0:T(8,128)(2,1)} async-done(((bf16[1,2,128,1024]{3,2,1,0:T(8,128)(2,1)}), bf16[1,2,128,256]{3,2,1,0:T(8,128)(2,1)}) %reduce-scatter.11.cloned.1.call-update) | async-done | bytes 131088 | tf_op jit(solution)/shard_map/reduce_scatter | solution.py:80
  600.7 21.5 %all-gather.24.cloned.1.call-done = bf16[1,16,128,256]{3,2,0,1:T(8,128)(2,1)} async-done(((bf16[1,2,128,256]{3,2,0,1:T(8,128)(2,1)}), bf16[1,16,128,256]{3,2,0,1:T(8,128)(2,1)}) %all-gather.24.cloned.1.call-update) | async-done | bytes 1048592 | tf_op jit(solution)/shard_map/all_gather | solution.py:139
  (568 shorter events, 220.6 us)
Async XLA Ops:
  7.2 52.9 %all-gather.28.cloned.1.call-start = ((), (), s32[]{:S(2)}) async-start(), calls=%async_computation.21 | async-start | bytes 5308416 | tf_op jit(solution)/shard_map/all_gather | solution.py:336
  9.8 117.7 %all-gather.30.cloned.1.call-start = ((), (), s32[]{:S(2)}) async-start(), calls=%async_computation.22 | async-start | bytes 5308416 | tf_op jit(solution)/shard_map/all_gather | solution.py:337
  10.5 149.1 %all-gather.14.cloned.1.call-start = ((), (), s32[]{:S(2)}) async-start(), calls=%async_computation.8 | async-start | bytes 2359296 | tf_op jit(solution)/shard_map/all_gather | solution.py:339
  10.6 4.7 collective-permute-start
  12.0 172.3 %all-reduce.9.cloned.1.call-start = ((), (), s32[]{:S(2)}) async-start(), calls=%async_computation.11 | async-start | bytes 262144 | tf_op jit(solution)/shard_map/psum | solution.py:361
  15.3 4.1 collective-permute-start.1
  40.6 19.2 %collective-permute-start.3 = (bf16[1,1,128,1024]{3,2,1,0:T(8,128)(2,1)S(1)}, bf16[1,1,128,1024]{3,2,1,0:T(8,128)(2,1)S(1)}, u32[]{:S(2)}, u32[]{:S(2)}) collective-permute-start(bf16[1,1,128,1024]{3,2,1,0:T(8,128)(2,1)S(1)} %get-tuple-element.506), channel_id=1, source_target_pairs={{0,4},{4,8},{8,12},{12,16},{16,20},{20,24},{24,28},{1,5},{5,9},{9,... | collective-permute-start | bytes 786440 | tf_op jit(solution)/shard_map/ppermute | solution.py:27
  41.9 17.9 %collective-permute-start.4 = (bf16[1,1,128,1024]{3,2,1,0:T(8,128)(2,1)S(1)}, bf16[1,1,128,1024]{3,2,1,0:T(8,128)(2,1)S(1)}, u32[]{:S(2)}, u32[]{:S(2)}) collective-permute-start(bf16[1,1,128,1024]{3,2,1,0:T(8,128)(2,1)S(1)} %get-tuple-element.507), channel_id=1, source_target_pairs={{4,0},{8,4},{12,8},{16,12},{20,16},{24,20},{28,24},{5,1},{9,5},{13... | collective-permute-start | bytes 786440 | tf_op jit(solution)/shard_map/ppermute | solution.py:29
  43.2 3.9 collective-permute-start.5
  47.1 9.0 %collective-permute-start.6 = (f32[1,2,256]{2,1,0:T(2,128)S(1)}, f32[1,2,256]{2,1,0:T(2,128)S(1)}, u32[]{:S(2)}, u32[]{:S(2)}) collective-permute-start(f32[1,2,256]{2,1,0:T(2,128)S(1)} %add.399), channel_id=1, source_target_pairs={{0,8},{4,12},{8,0},{12,4},{16,24},{20,28},{24,16},{28,20},{1,9},{5... | collective-permute-start | bytes 6152 | tf_op jit(solution)/shard_map/ppermute | solution.py:50
  73.8 135.3 %all-gather.22.cloned.1.call-start = ((), (), s32[]{:S(2)}) async-start(), calls=%async_computation.14 | async-start | bytes 1179648 | tf_op jit(solution)/shard_map/all_gather | solution.py:266
  93.2 33.0 %collective-permute-start.11 = (bf16[1,1,128,1024]{3,2,1,0:T(8,128)(2,1)S(1)}, bf16[1,1,128,1024]{3,2,1,0:T(8,128)(2,1)S(1)}, u32[]{:S(2)}, u32[]{:S(2)}) collective-permute-start(bf16[1,1,128,1024]{3,2,1,0:T(8,128)(2,1)S(1)} %get-tuple-element.504), channel_id=1, source_target_pairs={{0,4},{4,8},{8,12},{12,16},{16,20},{20,24},{24,28},{1,5},{5,9},{9,... | collective-permute-start | bytes 786440 | tf_op jit(solution)/shard_map/ppermute | solution.py:27
  94.5 31.7 %collective-permute-start.12 = (bf16[1,1,128,1024]{3,2,1,0:T(8,128)(2,1)S(1)}, bf16[1,1,128,1024]{3,2,1,0:T(8,128)(2,1)S(1)}, u32[]{:S(2)}, u32[]{:S(2)}) collective-permute-start(bf16[1,1,128,1024]{3,2,1,0:T(8,128)(2,1)S(1)} %get-tuple-element.505), channel_id=1, source_target_pairs={{4,0},{8,4},{12,8},{16,12},{20,16},{24,20},{28,24},{5,1},{9,5},{13... | collective-permute-start | bytes 786440 | tf_op jit(solution)/shard_map/ppermute | solution.py:29
  138.0 96.5 %all-gather.16.cloned.1.call-start = ((), (), s32[]{:S(2)}) async-start(), calls=%async_computation.9 | async-start | bytes 1179648 | tf_op jit(solution)/shard_map/all_gather | solution.py:192
  139.0 4.5 collective-permute-start.14
  163.6 96.6 %all-gather.18.cloned.1.call-start = ((), (), s32[]{:S(2)}) async-start(), calls=%async_computation.10 | async-start | bytes 1179648 | tf_op jit(solution)/shard_map/all_gather | solution.py:193
  164.4 134.8 %all-gather.20.cloned.1.call-start = ((), (), s32[]{:S(2)}) async-start(), calls=%async_computation.13 | async-start | bytes 1179648 | tf_op jit(solution)/shard_map/all_gather | solution.py:265
  214.7 125.4 %reduce-scatter.13.cloned.1.call-start = ((), (), s32[]{:S(2)}) async-start(), calls=%async_computation.15 | async-start | bytes 655360 | tf_op jit(solution)/shard_map/reduce_scatter | solution.py:80
  318.2 69.2 %reduce-scatter.15.cloned.1.call-start = ((), (), s32[]{:S(2)}) async-start(), calls=%async_computation.16 | async-start | bytes 655360 | tf_op jit(solution)/shard_map/reduce_scatter | solution.py:80
  345.4 4.5 collective-permute-start.16
  352.7 4.7 collective-permute-start.18
  364.6 82.8 %all-reduce.11.cloned.1.call-start = ((), (), s32[]{:S(2)}) async-start(), calls=%async_computation.20 | async-start | bytes 262144 | tf_op jit(solution)/shard_map/psum | solution.py:505
  367.2 113.8 %reduce-scatter.21.cloned.1.call-start = ((), (), s32[]{:S(2)}) async-start(), calls=%async_computation.24 | async-start | bytes 1179648
  369.4 137.7 %all-gather.26.cloned.1.call-start = ((), (), s32[]{:S(2)}) async-start(), calls=%async_computation.19 | async-start | bytes 1179648 | tf_op jit(solution)/shard_map/all_gather | solution.py:139
  400.4 4.8 collective-permute-start.23
  401.8 129.7 %reduce-scatter.17.cloned.1.call-start = ((), (), s32[]{:S(2)}) async-start(), calls=%async_computation.17 | async-start | bytes 655360 | tf_op jit(solution)/shard_map/reduce_scatter | solution.py:80
  413.7 160.9 %reduce-scatter.19.cloned.1.call-start = ((), (), s32[]{:S(2)}) async-start(), calls=%async_computation.23 | async-start | bytes 2359296
  440.8 14.0 %all-to-all-start.1 = ((bf16[1,2,128,1024]{2,1,0,3:T(2,128)(2,1)}), bf16[1,2,128,1024]{2,1,0,3:T(2,128)(2,1)}, u32[]{:S(2)}, u32[]{:S(2)}) async-start(bf16[1,2,128,1024]{2,1,0,3:T(2,128)(2,1)} %copy.226), calls=%async_computation.5 | async-start | bytes 1048576 | tf_op jit(solution)/shard_map/all_to_all | solution.py:137
  445.1 153.5 %reduce-scatter.11.cloned.1.call-start = ((), (), s32[]{:S(2)}) async-start(), calls=%async_computation.12 | async-start | bytes 655360 | tf_op jit(solution)/shard_map/reduce_scatter | solution.py:80
  446.6 175.6 %all-gather.24.cloned.1.call-start = ((), (), s32[]{:S(2)}) async-start(), calls=%async_computation.18 | async-start | bytes 1179648 | tf_op jit(solution)/shard_map/all_gather | solution.py:139
  447.0 35.1 %collective-permute-start.27 = (f32[1,2,256]{2,1,0:T(2,128)S(1)}, f32[1,2,256]{2,1,0:T(2,128)S(1)}, u32[]{:S(2)}, u32[]{:S(2)}) collective-permute-start(f32[1,2,256]{2,1,0:T(2,128)S(1)} %pad_maximum_fusion.18), channel_id=1, source_target_pairs={{0,4},{4,0},{8,12},{12,8},{16,20},{20,16},{24,28},{28,24},{1,5},{5... | collective-permute-start | bytes 6152 | tf_op jit(solution)/shard_map/ppermute | solution.py:50
  537.9 39.0 %collective-permute-start.26 = (f32[2,1,256]{2,1,0:T(1,128)}, f32[2,1,256]{2,1,0:T(1,128)}, u32[]{:S(2)}, u32[]{:S(2)}) collective-permute-start(f32[2,1,256]{2,1,0:T(1,128)} %fusion.380), channel_id=1, source_target_pairs={{0,16},{4,20},{8,24},{12,28},{16,0},{20,4},{24,8},{28,12},{1,17},{... | collective-permute-start | bytes 6152 | tf_op jit(solution)/shard_map/ppermute | solution.py:50
  (124 other events, 1809.4 us)
Sparse Core Ops, SparseCore 0:
  10.5 44.8 all-gather.27
  57.9 39.2 all-gather.29
  99.6 28.1 all-gather.13
  131.3 52.8 all-reduce.8
  186.2 22.9 all-gather.21
  211.1 23.4 all-gather.15
  236.7 23.4 all-gather.17
  262.8 23.4 all-gather.19
  318.3 21.7 reduce-scatter.12
  364.7 22.6 reduce-scatter.14
  390.7 51.5 all-reduce.10
  445.9 35.1 reduce-scatter.20
  483.5 23.4 all-gather.25
  509.8 21.6 reduce-scatter.16
  535.1 39.4 reduce-scatter.18
  576.9 21.6 reduce-scatter.10
  600.5 21.7 all-gather.23
